TPU v7x, 32 devices: a whole 2x2x4 slice. The times are simulated.
32 devices in a mesh: section: 2 (over y), dp: 4 (over x, core), tensor: 4 (over z).
Axes of the slice: x: 2, y: 2, z: 4, core: 2. Of those that a mesh axis runs over, the one named last changes fastest.
Arguments:
- inputs: bfloat16 [2, 1024, 12288], P('section', 'dp', 'tensor'), may hold values from -6 to 6
- queries: bfloat16 [2, 1024, 1024], P('section', 'dp', 'tensor'), may hold values from -8 to 8
- keys: bfloat16 [2, 1024, 1024], P('section', 'dp', 'tensor'), may hold values from -8 to 8
- w_value: bfloat16 [2, 12288, 1024], P('section', None, 'tensor'), may hold values from -0.0546875 to 0.0546875
- w_out: bfloat16 [2, 1024, 12288], P('section', 'tensor'), may hold values from -0.5 to 0.5
Outputs:
- next_inputs: bfloat16 [2, 1024, 12288], P('section', 'dp', 'tensor')
All inputs are finite; a program needn't handle non-finite values.
Results may differ from a plain program's by a relative error of at most 0.023.
Values may be sent and summed in bfloat16 or wider, within the bound.
A program may use at most 64 MiB of HBM per device.

v0:
```python
import functools

import jax
import jax.numpy as jnp
from jax import lax
from jax.experimental import pallas as pl
from jax.experimental.pallas import tpu as pltpu
from jax.sharding import PartitionSpec as P

HEAD_SIZE = 128
LEN = 256
V_SUB = 3
O_SHARES = (2, 2, 1, 1)
O_SUB, O_UNITS = len(O_SHARES), sum(O_SHARES)
WINDOW = 4
O_WINDOW = 3
GROUP = 4


def flip(index, bit):
    step = 2**bit
    return index + step - 2 * step * lax.rem(index // step, 2)


def flip_by(index, mask):
    for bit in range(mask.bit_length()):
        if mask >> bit & 1:
            index = flip(index, bit)
    return index


def moving_weights(
    n,
    activ_hbm, query_hbm, key_hbm, wv_hbm, wo_hbm, out_hbm,
    activ, residual, query, key, wv, wo, probs, own_part, part_out, part_in, own_context, context, result,
    local_sem, residual_sem, wv_send, wv_recv, wo_send, wo_recv, value_send, value_recv, context_send, context_recv, out_sem,
):
    section = lax.axis_index("section")
    dp = lax.axis_index("dp")
    z = lax.axis_index("tensor")
    length, cols = activ.shape
    quarter = cols // 4
    v_rows = quarter // V_SUB
    unit = quarter // O_UNITS
    o_start = [sum(O_SHARES[:sub]) * unit for sub in range(O_SUB)]
    o_cols = [share * unit for share in O_SHARES]
    core_peer = flip(dp, 0)
    chip_peer = flip(dp, 1)
    diagonal = flip(core_peer, 1)
    quarters = (dp, core_peer, chip_peer, diagonal)
    other = flip(section, 0)

    barrier = pltpu.get_barrier_semaphore()
    for slot in range(1, n):
        pl.semaphore_signal(barrier, inc=1, device_id=(section, dp, flip_by(z, slot)),
                            device_id_type=pl.DeviceIdType.MESH)
    targets = [(section, core_peer, z), (section, chip_peer, z)]
    targets += [(other, dp, flip_by(z, slot)) for slot in range(n)]
    for target in targets:
        pl.semaphore_signal(barrier, inc=1, device_id=target, device_id_type=pl.DeviceIdType.MESH)

    def remote(src, dst, send, recv, target):
        return pltpu.make_async_remote_copy(
            src_ref=src, dst_ref=dst, send_sem=send, recv_sem=recv,
            device_id=target, device_id_type=pl.DeviceIdType.MESH)

    own = pl.multiple_of(z * cols, cols)
    locals_ = [
        pltpu.make_async_copy(activ_hbm.at[0], activ, local_sem.at[0]),
        pltpu.make_async_copy(query_hbm.at[0], query, local_sem.at[1]),
        pltpu.make_async_copy(key_hbm.at[0], key, local_sem.at[2]),
        pltpu.make_async_copy(wv_hbm.at[0, pl.ds(own, cols), :], wv.at[0], local_sem.at[3]),
    ]
    pl.semaphore_wait(barrier, 2 * n + 1)

    pieces = [("v", 3, sub) for sub in range(V_SUB)]
    pieces += [("v", slot, sub) for sub in range(V_SUB) for slot in (2, 1)]
    n_value = len(pieces)
    pieces += [("o", slot, sub) for sub in range(O_SUB) for slot in (3, 2, 1)]
    pieces += [("o", 0, sub) for sub in range(O_SUB)]
    n_tensor = n_value + O_SUB * (n - 1)

    def v_at(slot, which, sub):
        rows = pl.ds(pl.multiple_of(which * quarter + sub * v_rows, v_rows), v_rows)
        return wv.at[slot, rows, :]

    def o_at(slot, which, sub):
        columns = pl.ds(pl.multiple_of(which * quarter + o_start[sub], unit), o_cols[sub])
        return wo.at[slot, :, columns]

    def copies(piece):
        kind, slot, sub = piece
        peer = flip_by(z, slot)
        if kind == "v":
            start = pl.multiple_of(peer * cols + dp * quarter + sub * v_rows, v_rows)
            source = wv_hbm.at[0, pl.ds(start, v_rows), :]
            at, send, recv, index, target = v_at, wv_send, wv_recv, slot - 1, (section, dp, peer)
        else:
            start = pl.multiple_of(peer * cols + dp * quarter + o_start[sub], unit)
            source = wo_hbm.at[0, :, pl.ds(start, o_cols[sub])]
            at, send, recv, index, target = o_at, wo_send, wo_recv, slot, (other, dp, peer)
        mine, far = at(slot, dp, sub), at(slot, chip_peer, sub)
        def sems(hop):
            return send.at[index, sub, hop], recv.at[index, sub, hop]
        return (
            remote(source, mine, *sems(0), target),
            remote(mine, mine, *sems(1), (section, core_peer, z)),
            remote(mine, mine, *sems(2), (section, chip_peer, z)),
            remote(far, far, *sems(3), (section, core_peer, z)),
        )

    plan = [copies(piece) for piece in pieces]
    for i in range(WINDOW):
        plan[i][0].start()
    for copy in locals_:
        copy.start()
    residual_copy = remote(activ_hbm.at[0], residual, residual_sem.at[0], residual_sem.at[1], (other, dp, z))
    for i in range(n_tensor, len(plan)):
        plan[i][0].start()
    residual_copy.start()

    def pass_on(i):
        plan[i][0].wait_recv()
        plan[i][2].start()
        plan[i][1].start()

    def relay(i):
        plan[i][2].wait_recv()
        plan[i][3].start()

    locals_[1].wait()
    locals_[2].wait()
    causal = lax.broadcasted_iota(jnp.int32, (LEN, LEN), 1) <= lax.broadcasted_iota(jnp.int32, (LEN, LEN), 0)
    scale = 1.0 / HEAD_SIZE**0.5
    heads = query.shape[1] // HEAD_SIZE
    blocks = [(start, head) for start in range(0, length, LEN) for head in range(heads)]
    for at, (start, head) in enumerate(blocks):
        rows, span = slice(start, start + LEN), slice(head * HEAD_SIZE, (head + 1) * HEAD_SIZE)
        scores = lax.dot_general(query[rows, span], key[rows, span], (((1,), (1,)), ((), ())),
                                 preferred_element_type=jnp.float32) * scale
        scores = jnp.where(causal, scores, -1e30)
        expo = jnp.exp(scores - jnp.max(scores, axis=-1, keepdims=True))
        probs[at] = (expo / jnp.sum(expo, axis=-1, keepdims=True)).astype(jnp.bfloat16)
    locals_[0].wait()
    locals_[3].wait()
    own_part[...] = jnp.dot(activ[...], wv[0], preferred_element_type=jnp.float32)

    near, across = flip_by(z, 1), flip_by(z, 2)
    value_copies = [
        remote(part_out.at[m], part_in.at[m], value_send.at[m], value_recv.at[m], (section, dp, to))
        for m, to in enumerate((near, across, near))]

    def send_value(slot):
        for i, (kind, at, _) in enumerate(pieces):
            if kind == "v" and at == slot:
                plan[i][1].wait_recv()
                plan[i][3].wait_recv()
        term = jnp.dot(activ[...], wv[slot], preferred_element_type=jnp.float32)
        if slot == 2:
            value_copies[0].wait_recv()
            term = term + part_in[0].astype(jnp.float32)
        part_out[3 - slot] = term.astype(jnp.bfloat16)
        value_copies[3 - slot].start()

    started = WINDOW
    sent = set()

    def advance(i):
        nonlocal started
        pass_on(i)
        if started < n_tensor:
            plan[i][0].wait_send()
            sent.add(i)
        ahead = i + 1 + (WINDOW if i + 1 < n_value else O_WINDOW)
        while started < min(ahead, n_tensor):
            plan[started][0].start()
            started += 1

    for i in range(n_value):
        advance(i)
        if i > 0:
            relay(i - 1)
        if i == V_SUB + 1:
            send_value(3)
    relay(n_value - 1)
    send_value(2)
    send_value(1)

    def piece_range(sub):
        first = n_value + sub * (n - 1)
        return [n_tensor + sub] + list(range(first, first + n - 1))

    def bring(sub, between=None):
        batch = piece_range(sub)
        pass_on(batch[0])
        for at, (before, i) in enumerate(zip(batch, batch[1:])):
            advance(i)
            relay(before)
            if between is not None:
                between(at)

    bring(0)
    value_copies[1].wait_recv()
    value_copies[2].wait_recv()
    total = own_part[...] + part_in[1].astype(jnp.float32) + part_in[2].astype(jnp.float32)
    values = total.astype(jnp.bfloat16)
    for at, (start, head) in enumerate(blocks):
        rows, span = slice(start, start + LEN), slice(head * HEAD_SIZE, (head + 1) * HEAD_SIZE)
        own_context[rows, span] = jnp.dot(
            probs[at], values[rows, span], preferred_element_type=jnp.float32).astype(jnp.bfloat16)

    routes = [(own_context, 2, (other, dp, across)), (own_context, 1, (other, dp, near)),
              (own_context, 0, (other, dp, z)), (context.at[2], 3, (section, dp, near))]
    context_copies = [
        remote(src, context.at[dst], context_send.at[m], context_recv.at[m], to)
        for m, (src, dst, to) in enumerate(routes)]
    for copy in context_copies[:3]:
        copy.start()
    relay(piece_range(0)[-1])
    bring(1)
    context_copies[0].wait_recv()
    context_copies[3].start()
    relay(piece_range(1)[-1])

    out_copies = []

    def chunk(sub, order):
        for i in piece_range(sub):
            if order == 1:
                plan[i][1].wait_recv()
            elif order == 3:
                plan[i][3].wait_recv()
        columns = pl.ds(pl.multiple_of(quarters[order] * quarter + o_start[sub], unit), o_cols[sub])
        total = residual[:, columns].astype(jnp.float32)
        for slot in range(n):
            total = total + jnp.dot(context[slot], wo[slot, :, columns],
                                    preferred_element_type=jnp.float32)
        result[:, columns] = total.astype(jnp.bfloat16)
        copy = pltpu.make_async_copy(result.at[:, columns], out_hbm.at[0, :, columns], out_sem.at[sub, order])
        copy.start()
        out_copies.append(copy)

    residual_copy.wait_recv()
    for copy in context_copies[1:]:
        copy.wait_recv()
    for order in range(4):
        chunk(0, order)
    for sub in range(2, O_SUB):
        def earlier(at):
            for order in {0: (0, 1), 1: (2, 3)}.get(at, ()):
                chunk(sub - 1, order)
        bring(sub, earlier)
        relay(piece_range(sub)[-1])
    for order in range(4):
        chunk(O_SUB - 1, order)

    for i, piece in enumerate(plan):
        if i not in sent:
            piece[0].wait_send()
        for copy in piece[1:]:
            copy.wait_send()
    for copy in value_copies + context_copies + [residual_copy]:
        copy.wait_send()
    for copy in out_copies:
        copy.wait()


def by_weights(n, inputs, queries, keys, w_value, w_out):
    length, cols = inputs.shape[1:]
    width = w_value.shape[2]
    bf16, dma = jnp.bfloat16, pltpu.SemaphoreType.DMA
    return pl.pallas_call(
        functools.partial(moving_weights, n),
        out_shape=jax.ShapeDtypeStruct(inputs.shape, bf16),
        in_specs=[pl.BlockSpec(memory_space=pl.ANY)] * 5,
        out_specs=pl.BlockSpec(memory_space=pl.ANY),
        scratch_shapes=[
            pltpu.VMEM((length, cols), bf16),
            pltpu.VMEM((length, cols), bf16),
            pltpu.VMEM((length, width), bf16),
            pltpu.VMEM((length, width), bf16),
            pltpu.VMEM((n, cols, width), bf16),
            pltpu.VMEM((n, width, cols), bf16),
            pltpu.VMEM((length // LEN * width // HEAD_SIZE, LEN, LEN), bf16),
            pltpu.VMEM((length, width), jnp.float32),
            pltpu.VMEM((n - 1, length, width), bf16),
            pltpu.VMEM((n - 1, length, width), bf16),
            pltpu.VMEM((length, width), bf16),
            pltpu.VMEM((n, length, width), bf16),
            pltpu.VMEM((length, cols), bf16),
            dma((4,)),
            dma((2,)),
            dma((n - 1, V_SUB, 4)),
            dma((n - 1, V_SUB, 4)),
            dma((n, O_SUB, 4)),
            dma((n, O_SUB, 4)),
            dma((n - 1,)),
            dma((n - 1,)),
            dma((n,)),
            dma((n,)),
            dma((O_SUB, 4)),
        ],
        compiler_params=pltpu.CompilerParams(
            collective_id=0, has_side_effects=True, vmem_limit_bytes=60 * 2**20),
        cost_estimate=pl.CostEstimate(
            flops=4 * length * cols * n * width, bytes_accessed=2 * 4 * n * cols * width,
            transcendentals=length * LEN * width // HEAD_SIZE),
        name="weights_to_activations",
    )(inputs, queries, keys, w_value, w_out)


def by_activations(inputs, queries, keys, w_value, w_out):
    activ = inputs[0]
    weight_v = w_value[0]
    weight_o = w_out[0]
    length = activ.shape[0]
    col_width = activ.shape[1]
    features_all = lax.all_gather(activ, "tensor", axis=1, tiled=True)
    values = jnp.dot(features_all, weight_v, preferred_element_type=jnp.float32)
    values = values.astype(jnp.bfloat16)
    heads_here = weight_v.shape[1] // HEAD_SIZE
    query_rows = queries[0].reshape(length // LEN, LEN, heads_here, HEAD_SIZE)
    key_rows = keys[0].reshape(length // LEN, LEN, heads_here, HEAD_SIZE)
    value_rows = values.reshape(length // LEN, LEN, heads_here, HEAD_SIZE)
    scores = jnp.einsum(
        "bqhd,bkhd->bhqk", query_rows, key_rows, preferred_element_type=jnp.float32
    ) / jnp.sqrt(jnp.float32(HEAD_SIZE))
    rows = lax.broadcasted_iota(jnp.int32, (LEN, LEN), 0)
    cols = lax.broadcasted_iota(jnp.int32, (LEN, LEN), 1)
    scores = jnp.where((cols <= rows)[None, None], scores, jnp.float32(-1e30))
    top = jnp.max(scores, axis=-1, keepdims=True)
    expo = jnp.exp(scores - top)
    probs = (expo / jnp.sum(expo, axis=-1, keepdims=True)).astype(jnp.bfloat16)
    context = jnp.einsum(
        "bhqk,bkhd->bqhd", probs, value_rows, preferred_element_type=jnp.float32
    ).astype(jnp.bfloat16)
    context = context.reshape(length, heads_here * HEAD_SIZE)
    partial_term = jnp.dot(context, weight_o, preferred_element_type=jnp.float32)
    total = lax.psum_scatter(
        partial_term.astype(jnp.bfloat16), "tensor", scatter_dimension=1, tiled=True)
    result = (total.astype(jnp.float32) + activ.astype(jnp.float32)).astype(jnp.bfloat16)
    size = lax.axis_size("section")
    return lax.ppermute(result, "section", [(i, i ^ 1) for i in range(size)])[None]


def solution(mesh):
    n = mesh.shape["tensor"]

    def on_device(inputs, queries, keys, w_value, w_out):
        length, cols = inputs.shape[1:]
        width = w_value.shape[2]
        weights_smaller = n * width <= mesh.shape["dp"] * length
        divides = (cols % (4 * 128 * O_UNITS) == 0 and cols % (4 * 16 * V_SUB) == 0
                   and length % LEN == 0 and n == GROUP and mesh.shape["dp"] == 4)
        if weights_smaller and divides:
            return by_weights(n, inputs, queries, keys, w_value, w_out)
        return by_activations(inputs, queries, keys, w_value, w_out)

    return jax.shard_map(
        on_device,
        mesh=mesh,
        in_specs=(
            P("section", "dp", "tensor"),
            P("section", "dp", "tensor"),
            P("section", "dp", "tensor"),
            P("section", None, "tensor"),
            P("section", "tensor", None),
        ),
        out_specs=P("section", "dp", "tensor"),
        check_vma=False,
    )
```

profile of v0, /device:TPU:0, one launch (start us, length us, event | category | flops | bytes accessed | tf_op | source)
XLA Modules:
  0.0 114.9 jit_solution(10201203811927339483)
XLA Ops:
  0.0 112.2 %weights_to_activations.1 = bf16[1,256,3072]{2,1,0:T(8,128)(2,1)} custom-call(bf16[1,256,3072]{2,1,0:T(8,128)(2,1)} %activ_hbm.1, bf16[1,256,256]{2,1,0:T(8,128)(2,1)} %query_hbm.1, bf16[1,256,256]{2,1,0:T(8,128)(2,1)} %key_hbm.1, bf16[1,12288,256]{2,1,0:T(8,128)(2,1)} %wv_hbm.1, bf16[1,256,12288]{2,1,0:T(8,128)(2,1)} %wo_hbm.1), custom_call_target="tpu_custom_call" | custom-call | flops 3221225472 | bytes 25165824 | tf_op jit(solution)/shard_map/weights_to_activations/pallas_call | solution.py:272
  112.2 2.7 %copy.7 = bf16[1,256,3072]{2,1,0:T(8,128)(2,1)} copy(bf16[1,256,3072]{2,1,0:T(8,128)(2,1)} %weights_to_activations.1) | data formatting | bytes 3145728
where the time goes:
time: 115 us
  Pallas kernels  112 us (97%)
  local copies, waits for them, and re-layouts  2.65 us (2%)
    pallas_call x1, Pallas kernels, by_weights(): pl.pallas_call(functools.partial(moving_weights, n), out_shape=jax.ShapeD...  112 us
    unnamed x1, local copies, waits for them, and re-layouts  2.65 us

commit v1 on v0

--- a/solution.py
+++ b/solution.py
@@ -13,7 +13,7 @@
 O_SHARES = (2, 2, 1, 1)
 O_SUB, O_UNITS = len(O_SHARES), sum(O_SHARES)
 WINDOW = 4
-O_WINDOW = 3
+O_WINDOW = 6
 GROUP = 4
 
 
@@ -240,17 +240,21 @@
         copy.start()
         out_copies.append(copy)
 
-    residual_copy.wait_recv()
-    for copy in context_copies[1:]:
-        copy.wait_recv()
-    for order in range(4):
-        chunk(0, order)
     for sub in range(2, O_SUB):
         def earlier(at):
             for order in {0: (0, 1), 1: (2, 3)}.get(at, ()):
                 chunk(sub - 1, order)
-        bring(sub, earlier)
+        bring(sub, earlier if sub > 2 else None)
+        if sub == 2:
+            residual_copy.wait_recv()
+            for copy in context_copies[1:]:
+                copy.wait_recv()
+            for order in range(4):
+                chunk(0, order)
         relay(piece_range(sub)[-1])
+        if sub == 2:
+            for order in range(4):
+                chunk(1, order)
     for order in range(4):
         chunk(O_SUB - 1, order)
 

time: 115 us -> 112 us (0.974)
  Pallas kernels: 112 us -> 109 us
    pallas_call x1, Pallas kernels: 112 us -> 109 us  [by_weights(): pl.pallas_call(functools.partial(moving_weights, n), out_shape=jax.ShapeD...]
where the time goes in v1:
time: 112 us
  Pallas kernels  109 us (97%)
  local copies, waits for them, and re-layouts  2.65 us (2%)
    pallas_call x1, Pallas kernels, by_weights(): pl.pallas_call(functools.partial(moving_weights, n), out_shape=jax.ShapeD...  109 us
    unnamed x1, local copies, waits for them, and re-layouts  2.65 us

profile of v1, /device:TPU:0, one launch (start us, length us, event | category | flops | bytes accessed | tf_op | source)
XLA Modules:
  0.0 111.6 jit_solution(905448528252571004)
XLA Ops:
  0.0 108.9 %weights_to_activations.1 = bf16[1,256,3072]{2,1,0:T(8,128)(2,1)} custom-call(bf16[1,256,3072]{2,1,0:T(8,128)(2,1)} %activ_hbm.1, bf16[1,256,256]{2,1,0:T(8,128)(2,1)} %query_hbm.1, bf16[1,256,256]{2,1,0:T(8,128)(2,1)} %key_hbm.1, bf16[1,12288,256]{2,1,0:T(8,128)(2,1)} %wv_hbm.1, bf16[1,256,12288]{2,1,0:T(8,128)(2,1)} %wo_hbm.1), custom_call_target="tpu_custom_call" | custom-call | flops 3221225472 | bytes 25165824 | tf_op jit(solution)/shard_map/weights_to_activations/pallas_call | solution.py:276
  108.9 2.7 %copy.7 = bf16[1,256,3072]{2,1,0:T(8,128)(2,1)} copy(bf16[1,256,3072]{2,1,0:T(8,128)(2,1)} %weights_to_activations.1) | data formatting | bytes 3145728

commit v2 on v1

--- a/solution.py
+++ b/solution.py
@@ -13,7 +13,8 @@
 O_SHARES = (2, 2, 1, 1)
 O_SUB, O_UNITS = len(O_SHARES), sum(O_SHARES)
 WINDOW = 4
-O_WINDOW = 6
+FEW = 2
+O_WINDOW = 5
 GROUP = 4
 
 
@@ -165,19 +166,21 @@
     started = WINDOW
     sent = set()
 
-    def advance(i):
+    def start_until(end):
         nonlocal started
+        while started < min(end, n_tensor):
+            plan[started][0].start()
+            started += 1
+
+    def advance(i, ahead):
         pass_on(i)
         if started < n_tensor:
             plan[i][0].wait_send()
             sent.add(i)
-        ahead = i + 1 + (WINDOW if i + 1 < n_value else O_WINDOW)
-        while started < min(ahead, n_tensor):
-            plan[started][0].start()
-            started += 1
+        start_until(i + 1 + ahead)
 
     for i in range(n_value):
-        advance(i)
+        advance(i, min(WINDOW, n_value + FEW - i - 1))
         if i > 0:
             relay(i - 1)
         if i == V_SUB + 1:
@@ -190,16 +193,16 @@
         first = n_value + sub * (n - 1)
         return [n_tensor + sub] + list(range(first, first + n - 1))
 
-    def bring(sub, between=None):
+    def bring(sub, ahead, between=None):
         batch = piece_range(sub)
         pass_on(batch[0])
         for at, (before, i) in enumerate(zip(batch, batch[1:])):
-            advance(i)
+            advance(i, ahead)
             relay(before)
             if between is not None:
                 between(at)
 
-    bring(0)
+    bring(0, FEW)
     value_copies[1].wait_recv()
     value_copies[2].wait_recv()
     total = own_part[...] + part_in[1].astype(jnp.float32) + part_in[2].astype(jnp.float32)
@@ -216,10 +219,11 @@
         for m, (src, dst, to) in enumerate(routes)]
     for copy in context_copies[:3]:
         copy.start()
+    start_until(n_value + n - 1 + O_WINDOW)
     relay(piece_range(0)[-1])
-    bring(1)
     context_copies[0].wait_recv()
     context_copies[3].start()
+    bring(1, O_WINDOW)
     relay(piece_range(1)[-1])
 
     out_copies = []
@@ -244,7 +248,7 @@
         def earlier(at):
             for order in {0: (0, 1), 1: (2, 3)}.get(at, ()):
                 chunk(sub - 1, order)
-        bring(sub, earlier if sub > 2 else None)
+        bring(sub, O_WINDOW, earlier if sub > 2 else None)
         if sub == 2:
             residual_copy.wait_recv()
             for copy in context_copies[1:]:

time: 112 us -> 121 us (1.080)
  Pallas kernels: 109 us -> 118 us
    pallas_call x1, Pallas kernels: 109 us -> 118 us  [by_weights(): pl.pallas_call(functools.partial(moving_weights, n), out_shape=jax.ShapeD...]
where the time goes in v2:
time: 121 us
  Pallas kernels  118 us (98%)
  local copies, waits for them, and re-layouts  2.65 us (2%)
    pallas_call x1, Pallas kernels, by_weights(): pl.pallas_call(functools.partial(moving_weights, n), out_shape=jax.ShapeD...  118 us
    unnamed x1, local copies, waits for them, and re-layouts  2.65 us

profile of v2, /device:TPU:0, one launch (start us, length us, event | category | flops | bytes accessed | tf_op | source)
XLA Modules:
  0.0 121.1 jit_solution(16958454082123421823)
XLA Ops:
  0.0 118.4 %weights_to_activations.1 = bf16[1,256,3072]{2,1,0:T(8,128)(2,1)} custom-call(bf16[1,256,3072]{2,1,0:T(8,128)(2,1)} %activ_hbm.1, bf16[1,256,256]{2,1,0:T(8,128)(2,1)} %query_hbm.1, bf16[1,256,256]{2,1,0:T(8,128)(2,1)} %key_hbm.1, bf16[1,12288,256]{2,1,0:T(8,128)(2,1)} %wv_hbm.1, bf16[1,256,12288]{2,1,0:T(8,128)(2,1)} %wo_hbm.1), custom_call_target="tpu_custom_call" | custom-call | flops 3221225472 | bytes 25165824 | tf_op jit(solution)/shard_map/weights_to_activations/pallas_call | solution.py:280
  118.5 2.7 %copy.7 = bf16[1,256,3072]{2,1,0:T(8,128)(2,1)} copy(bf16[1,256,3072]{2,1,0:T(8,128)(2,1)} %weights_to_activations.1) | data formatting | bytes 3145728
